TPU v7x, 512 devices: a whole 4x8x8 slice. The times are simulated.
512 devices in a mesh: seq: 16 (over y, core), wide: 32 (over z, x).
Axes of the slice: x: 4, y: 8, z: 8, core: 2. Of those that a mesh axis runs over, the one named last changes fastest.
Arguments:
- out_gate: bfloat16 [65536, 4096], P(('seq', 'wide')), may hold values from -6 to 6
- in_gate: bfloat16 [65536, 4096], P(('seq', 'wide')), may hold values from -6 to 6
- values: bfloat16 [65536, 4096], P(('seq', 'wide')), may hold values from -6 to 6
- filter_taps: bfloat16 [4096, 4096], P('seq', 'wide'), may hold values from -0.09375 to 0.09375
- skip_gain: float32 [4096], P('wide'), may hold values from 0.5 to 1.5
Outputs:
- mixed: bfloat16 [65536, 4096], P(('seq', 'wide'))
All inputs are finite; a program needn't handle non-finite values.
Results may differ from a plain program's by a relative error of at most 0.0065.
Values may be sent and summed in bfloat16 or wider, within the bound.
A program may use at most 64 MiB of HBM per device.

v0:
```python
import math

import jax
import jax.numpy as jnp
from jax import lax
from jax.sharding import PartitionSpec as P

PRECISE = lax.Precision.HIGH


def passed_along(value, axis, by):
    length = lax.axis_size(axis)
    pairs = [(i, i + by) for i in range(length) if 0 <= i + by < length]
    return lax.ppermute(value, axis, pairs)


def phase_table(first_count, second_count, modulus):
    first_index = lax.iota(jnp.int32, first_count)
    second_index = lax.iota(jnp.int32, second_count)
    product = first_index[:, None] * second_index[None, :] % modulus
    angle_table = product.astype(jnp.float32) * (-2.0 * math.pi / modulus)
    return (jnp.cos(angle_table), jnp.sin(angle_table))


def column_block(column_count, orientation):
    cosine_table, sine_table = phase_table(column_count, column_count, column_count)
    upper_rows = jnp.stack([cosine_table, orientation * sine_table], axis=1)
    bottom = jnp.stack([-orientation * sine_table, cosine_table], axis=1)
    return jnp.stack([upper_rows, bottom], axis=0)


def rotate(pair_parts, row_count, column_count, padded_size, orientation):
    twist_cosine, twist_sine = phase_table(row_count, column_count, padded_size)
    twist_sine = orientation * twist_sine
    real_part = pair_parts[0] * twist_cosine[:, :, None] - pair_parts[1] * twist_sine[:, :, None]
    imaginary = pair_parts[0] * twist_sine[:, :, None] + pair_parts[1] * twist_cosine[:, :, None]
    return jnp.stack([real_part, imaginary], axis=0)


def causal_filter(signal, tap_columns, padded_size):
    column_count = 64
    channels = signal.shape[1]
    rows_used = max(signal.shape[0], tap_columns.shape[0]) // column_count
    row_count = padded_size // column_count
    half_rows = row_count // 2 + 1
    cosine_first, sine_first = phase_table(row_count, rows_used, row_count)
    first_table = jnp.concatenate(
        [
            jnp.concatenate([cosine_first, -sine_first], axis=1),
            jnp.concatenate([sine_first, cosine_first], axis=1),
        ],
        axis=0,
    )
    joined = jnp.concatenate(
        [
            signal.reshape(rows_used, column_count * channels),
            tap_columns.reshape(rows_used, column_count * channels),
        ],
        axis=0,
    )
    first = jnp.dot(first_table, joined, precision=PRECISE).reshape(
        2, row_count, column_count, channels
    )
    turned = rotate(first, row_count, column_count, padded_size, 1.0)
    spectrum = jnp.einsum(
        "panc,pnqk->qakc", turned, column_block(column_count, 1.0), precision=PRECISE
    )
    kept = spectrum[:, :half_rows]
    zero_row = jnp.roll(jnp.flip(spectrum[:, :1], axis=2), 1, axis=2)
    mirrored = jnp.flip(spectrum[:, row_count // 2 :], axis=(1, 2))
    partner = jnp.concatenate([zero_row, mirrored], axis=1)
    signal_real = 0.5 * (kept[0] + partner[0])
    signal_imag = 0.5 * (kept[1] - partner[1])
    taps_real = 0.5 * (kept[1] + partner[1])
    taps_imag = 0.5 * (partner[0] - kept[0])
    product_real = signal_real * taps_real - signal_imag * taps_imag
    product_imag = signal_real * taps_imag + signal_imag * taps_real
    product = jnp.stack([product_real, product_imag], axis=0)
    mixed = jnp.einsum(
        "pakc,pkqn->qanc", product, column_block(column_count, -1.0), precision=PRECISE
    )
    returned = rotate(mixed, half_rows, column_count, padded_size, -1.0)
    cosine_last, sine_last = phase_table(row_count, half_rows, row_count)
    frequency = lax.iota(jnp.int32, half_rows)
    weights = jnp.where((frequency == 0) | (frequency == row_count // 2), 1.0, 2.0).astype(
        jnp.float32
    )
    last_table = (
        jnp.concatenate([cosine_last * weights[None, :], sine_last * weights[None, :]], axis=1)
        / padded_size
    )
    flattened = returned.reshape(2 * half_rows, column_count * channels)
    result = jnp.dot(last_table, flattened, precision=PRECISE)
    return result.reshape(padded_size, channels)


def local(out_gate, in_gate, values, filter_taps, skip_gain):
    gated_values = (in_gate.astype(jnp.float32) * values.astype(jnp.float32)).astype(jnp.bfloat16)
    all_taps = lax.all_gather(filter_taps, "seq", axis=0, tiled=True)
    by_channel = lax.all_to_all(gated_values, "wide", split_axis=1, concat_axis=0, tiled=True)
    group_length = by_channel.shape[0]
    tap_count = all_taps.shape[0]
    linear = causal_filter(by_channel, all_taps, group_length + tap_count)
    own_part = linear[:group_length]
    future = linear[group_length:]
    incoming = passed_along(future.astype(jnp.bfloat16), "seq", 1).astype(future.dtype)
    convolved = own_part + incoming
    filtered = (convolved + skip_gain[None, :] * by_channel.astype(jnp.float32)).astype(
        jnp.bfloat16
    )
    returned = lax.all_to_all(filtered, "wide", split_axis=0, concat_axis=1, tiled=True)
    return (out_gate.astype(jnp.float32) * returned.astype(jnp.float32)).astype(jnp.bfloat16)


def solution(mesh):
    in_specs = (
        P(("seq", "wide"), None),
        P(("seq", "wide"), None),
        P(("seq", "wide"), None),
        P("seq", "wide"),
        P("wide"),
    )
    out_specs = P(("seq", "wide"), None)
    return jax.shard_map(local, mesh=mesh, in_specs=in_specs, out_specs=out_specs, check_vma=False)
```

profile of v0, /device:TPU:16, one launch (start us, length us, event | category | flops | bytes accessed | tf_op | source)
XLA Modules:
  0.0 183.6 jit_solution(17083957285483094685)
XLA Ops:
  6.5 1.6 copy.25
  8.2 1.6 copy.26
  9.8 0.3 multiply_convert_fusion
  10.1 1.3 copy.27
  11.4 13.2 %all-to-all-start = ((bf16[128,32,128]{2,0,1:T(8,128)(2,1)}), bf16[128,32,128]{2,0,1:T(8,128)(2,1)S(1)}, u32[]{:S(2)}, u32[]{:S(2)}) async-start(bf16[128,32,128]{2,0,1:T(8,128)(2,1)} %copy.27), calls=%async_computation | async-start | bytes 2097152 | tf_op jit(solution)/shard_map/all_to_all | solution.py:100
  24.5 0.0 all-gather.2.cloned.1.call-start
  24.6 0.7 all-gather.2.cloned.1.call-update
  25.3 0.1 fusion.77
  25.4 0.3 fusion.74
  25.7 0.1 broadcast_multiply_fusion
  25.9 0.8 sine_multiply_fusion.1
  26.7 0.9 fusion.69
  27.6 0.3 fusion.67
  27.8 0.7 fusion.38
  28.5 0.3 cosine_multiply_fusion
  28.8 39.4 %all-gather.2.cloned.1.call-done = bf16[4096,128]{1,0:T(8,128)(2,1)} async-done(((bf16[256,128]{1,0:T(8,128)(2,1)}), bf16[4096,128]{1,0:T(8,128)(2,1)}) %all-gather.2.cloned.1.call-update) | async-done | bytes 1048592 | tf_op jit(solution)/shard_map/all_gather | solution.py:99
  68.2 1.5 reshape.233
  69.7 0.0 all-to-all-done
  69.8 0.5 reshape.232
  70.3 3.4 %fusion.16 = f32[256,8192]{1,0:T(8,128)S(1)} fusion(bf16[64,8192]{1,0:T(8,128)(2,1)S(1)} %reshape.233, bf16[64,8192]{1,0:T(8,128)(2,1)S(1)} %reshape.232, f32[128,64]{1,0:T(8,128)} %get-tuple-element.22, f32[128,64]{1,0:T(8,128)S(1)} %get-tuple-element.21, f32[128,64]{1,0:T(8,128)S(1)} %fusion.74), kind=kOutput, calls=%fused_computation.31 | convolution fusion | flops 1614905344 | bytes 10584064 | tf_op jit(solution)/shard_map/dot_general | solution.py:61
  73.6 0.9 slice_bitcast_fusion.1
  74.5 0.7 copy.43
  75.3 0.7 copy.42
  76.0 0.0 copy-start.6
  76.0 0.0 copy-start.7
  76.1 2.5 %fusion.8 = (f32[1,128,64,128]{3,2,0,1:T(8,128)S(1)}, f32[1,128,64,128]{3,2,0,1:T(8,128)S(1)}) fusion(f32[128,64]{1,0:T(8,128)S(1)} %get-tuple-element.23, f32[128,64]{1,0:T(8,128)S(1)} %get-tuple-element.24, f32[1,128,64,128]{3,2,1,0:T(8,128)S(1)} %bitcast.110, f32[1,128,64,128]{3,2,1,0:T(8,128)S(1)} %bitcast.111), kind=kLoop, calls=%fused_computation.13 | loop fusion | flops 6291456 | bytes 16842752 | tf_op jit(solution)/shard_map/sub | solution.py:35
  78.5 0.0 copy-done.6
  78.5 0.0 copy-done.7
  78.6 4.3 %fusion.12 = f32[2,128,64,128]{3,2,1,0:T(8,128)S(1)} fusion(f32[1,128,64,128]{3,2,0,1:T(8,128)S(1)} %get-tuple-element.8, f32[1,128,64,128]{3,2,0,1:T(8,128)S(1)} %get-tuple-element.7, f32[1,64,2,64]{1,3,0,2:T(8,128)S(1)} %copy-done.6, f32[1,64,2,64]{1,3,0,2:T(8,128)S(1)} %copy-done.7), kind=kOutput, calls=%fused_computation.20 | convolution fusion | flops 1612726272 | bytes 16842752 | tf_op jit(solution)/shard_map/panc,pnqk->qakc/dot_general | solution.py:65
  82.9 0.0 copy-start
  82.9 2.8 %slice.86 = f32[2,64,64,128]{3,2,1,0:T(8,128)} slice(f32[2,128,64,128]{3,2,1,0:T(8,128)S(1)} %fusion.12), slice={[0:2], [64:128], [0:64], [0:128]} | slice | bytes 8388608 | tf_op jit(solution)/shard_map/slice | solution.py:70
  85.7 1.7 copy-done
  87.4 6.6 %rev.6 = f32[2,64,64,128]{3,2,1,0:T(8,128)} reverse(f32[2,64,64,128]{3,2,1,0:T(8,128)} %slice.86), dimensions={1,2} | reverse | bytes 8388608 | tf_op jit(solution)/shard_map/jit(_flip)/rev | solution.py:70
  94.1 0.0 copy-start.1
  94.1 2.9 %pad_maximum_fusion = f32[2,65,64,128]{3,2,1,0:T(8,128)S(1)} fusion(f32[2,64,64,128]{3,2,1,0:T(8,128)} %rev.6, f32[2,1,63,128]{3,2,1,0:T(8,128)S(1)} %slice.71, f32[2,1,1,128]{3,2,1,0:T(1,128)S(1)} %slice.84), kind=kLoop, calls=%fused_computation.4 | loop fusion | flops 2129920 | bytes 8519680 | tf_op jit(solution)/shard_map/concatenate | solution.py:71
  97.0 1.7 copy-done.1
  98.7 1.5 multiply_subtract_fusion.1
  100.2 0.0 copy-done.4
  100.3 0.0 copy-done.5
  100.3 0.0 copy-start.8
  100.3 0.0 copy-start.9
  100.3 2.2 %fusion.13 = f32[2,65,64,128]{3,2,1,0:T(8,128)S(1)} fusion(f32[1,65,64,128]{3,2,1,0:T(8,128)S(1)} %get-tuple-element.6, f32[1,65,64,128]{3,2,1,0:T(8,128)S(1)} %get-tuple-element.5, f32[1,64,2,64]{1,3,2,0:T(8,128)S(1)} %copy-done.5, f32[1,64,2,64]{1,3,2,0:T(8,128)S(1)} %copy-done.4), kind=kOutput, calls=%fused_computation.21 | convolution fusion | flops 818970624 | bytes 8585216 | tf_op jit(solution)/shard_map/pakc,pkqn->qanc/dot_general | solution.py:79
  102.5 0.0 copy-done.8
  102.5 0.0 copy-done.9
  102.5 1.4 multiply_subtract_fusion
  104.0 0.6 pad_maximum_fusion.2
  104.6 0.3 pad.29
  104.9 3.6 %copy.44 = f32[17,8,64,128]{3,1,2,0:T(8,128)S(1)} copy(f32[17,8,64,128]{3,2,1,0:T(8,128)S(1)} %bitcast.108) | data formatting | bytes 8912896
  108.5 2.1 %fusion.23 = f32[128,8192]{1,0:T(8,128)S(1)} fusion(f32[130,8192]{1,0:T(8,128)S(1)} %bitcast.107, f32[128,65]{1,0:T(8,128)S(1)} %get-tuple-element.20, f32[128,65]{1,0:T(8,128)S(1)} %get-tuple-element.19), kind=kOutput, calls=%fused_computation.42 | convolution fusion | flops 817922560 | bytes 8520704 | tf_op jit(solution)/shard_map/dot_general | solution.py:93
  110.6 0.0 copy-start.2
  110.6 1.9 %copy-done.2 = f32[128,8192]{1,0:T(8,128)} copy-done((f32[128,8192]{1,0:T(8,128)}, f32[128,8192]{1,0:T(8,128)S(1)}, u32[]{:S(2)}) %copy-start.2) | copy-done | bytes 4194328
  112.5 1.1 slice.141
  113.6 2.5 %convert_element_type.128 = bf16[4096,128]{1,0:T(8,128)(2,1)} reshape(bf16[64,8192]{1,0:T(8,128)(2,1)} %slice.141) | data formatting | bytes 2097152 | tf_op jit(solution)/shard_map/convert_element_type | solution.py:106
  116.1 2.3 %collective-permute-start = (bf16[4096,128]{1,0:T(8,128)(2,1)}, bf16[4096,128]{1,0:T(8,128)(2,1)}, u32[]{:S(2)}, u32[]{:S(2)}) collective-permute-start(bf16[4096,128]{1,0:T(8,128)(2,1)} %convert_element_type.128), channel_id=1, source_target_pairs={{0,32},{32,64},{64,96},{96,128},{128,160},{160,192},{192,224},{224... | collective-permute-start | bytes 3145736 | tf_op jit(solution)/shard_map/ppermute | solution.py:14
  118.4 0.0 slice-done
  118.4 1.5 slice.79
  119.9 12.7 %collective-permute-done = bf16[4096,128]{1,0:T(8,128)(2,1)} collective-permute-done((bf16[4096,128]{1,0:T(8,128)(2,1)}, bf16[4096,128]{1,0:T(8,128)(2,1)}, u32[]{:S(2)}, u32[]{:S(2)}) %collective-permute-start) | collective-permute-done | bytes 1048608 | tf_op jit(solution)/shard_map/ppermute | solution.py:14
  132.7 3.2 %fusion.22 = bf16[4096,128]{1,0:T(8,128)(2,1)} fusion(f32[4096,128]{1,0:T(8,128)} %slice.79, bf16[4096,128]{1,0:T(8,128)(2,1)} %collective-permute-done, bf16[128,32,128]{2,0,1:T(8,128)(2,1)S(1)} %all-to-all-done, f32[128]{0:T(128)S(1)} %copy-done.10), kind=kLoop, calls=%fused_computation.39 | loop fusion | flops 3145728 | bytes 5243392 | tf_op jit(solution)/shard_map/convert_element_type | solution.py:108
  135.9 10.2 %all-to-all-start.1 = ((bf16[32,128,128]{2,1,0:T(8,128)(2,1)}), bf16[32,128,128]{2,1,0:T(8,128)(2,1)S(1)}, u32[]{:S(2)}, u32[]{:S(2)}) async-start(bf16[32,128,128]{2,1,0:T(8,128)(2,1)} %bitcast.25), calls=%async_computation.1 | async-start | bytes 2097152 | tf_op jit(solution)/shard_map/all_to_all | solution.py:111
  146.2 0.7 copy.23
  146.9 27.7 %all-to-all-done.1 = bf16[32,128,128]{2,1,0:T(8,128)(2,1)S(1)} async-done(((bf16[32,128,128]{2,1,0:T(8,128)(2,1)}), bf16[32,128,128]{2,1,0:T(8,128)(2,1)S(1)}, u32[]{:S(2)}, u32[]{:S(2)}) %all-to-all-start.1) | async-done | bytes 1048608 | tf_op jit(solution)/shard_map/all_to_all | solution.py:111
  174.5 0.7 copy.34
  175.2 0.3 fusion.20
  175.5 1.3 copy.35
  (11 shorter events, 0.1 us)
Async XLA Ops:
  11.4 58.4 %all-to-all-start = ((bf16[128,32,128]{2,0,1:T(8,128)(2,1)}), bf16[128,32,128]{2,0,1:T(8,128)(2,1)S(1)}, u32[]{:S(2)}, u32[]{:S(2)}) async-start(bf16[128,32,128]{2,0,1:T(8,128)(2,1)} %copy.27), calls=%async_computation | async-start | bytes 2097152 | tf_op jit(solution)/shard_map/all_to_all | solution.py:100
  24.5 43.7 %all-gather.2.cloned.1.call-start = ((), (), s32[]{:S(2)}) async-start(), calls=%async_computation.2 | async-start | bytes 1114112 | tf_op jit(solution)/shard_map/all_gather | solution.py:99
  76.0 2.5 %copy-start.6 = (f32[1,64,2,64]{1,3,0,2:T(8,128)S(1)}, f32[1,64,2,64]{1,3,0,2:T(8,128)}, u32[]{:S(2)}) copy-start(f32[1,64,2,64]{1,3,0,2:T(8,128)} %get-tuple-element.14) | copy-start | bytes 98308
  76.0 2.5 %copy-start.7 = (f32[1,64,2,64]{1,3,0,2:T(8,128)S(1)}, f32[1,64,2,64]{1,3,0,2:T(8,128)}, u32[]{:S(2)}) copy-start(f32[1,64,2,64]{1,3,0,2:T(8,128)} %get-tuple-element.17) | copy-start | bytes 98308
  82.9 4.5 %copy-start = (f32[2,128,64,128]{3,2,1,0:T(8,128)}, f32[2,128,64,128]{3,2,1,0:T(8,128)S(1)}, u32[]{:S(2)}) copy-start(f32[2,128,64,128]{3,2,1,0:T(8,128)S(1)} %fusion.12) | copy-start | bytes 25165828
  94.1 4.6 %copy-start.1 = (f32[2,128,64,128]{3,2,1,0:T(8,128)S(1)}, f32[2,128,64,128]{3,2,1,0:T(8,128)}, u32[]{:S(2)}) copy-start(f32[2,128,64,128]{3,2,1,0:T(8,128)} %copy-done) | copy-start | bytes 25165828
  98.7 1.5 copy-start.4
  98.7 1.5 copy-start.5
  100.3 2.2 %copy-start.8 = (f32[65,64]{1,0:T(8,128)S(1)}, f32[65,64]{1,0:T(8,128)}, u32[]{:S(2)}) copy-start(f32[65,64]{1,0:T(8,128)} %get-tuple-element.27) | copy-start | bytes 49924
  100.3 2.2 %copy-start.9 = (f32[65,64]{1,0:T(8,128)S(1)}, f32[65,64]{1,0:T(8,128)}, u32[]{:S(2)}) copy-start(f32[65,64]{1,0:T(8,128)} %get-tuple-element.28) | copy-start | bytes 49924
  110.6 2.0 %copy-start.2 = (f32[128,8192]{1,0:T(8,128)}, f32[128,8192]{1,0:T(8,128)S(1)}, u32[]{:S(2)}) copy-start(f32[128,8192]{1,0:T(8,128)S(1)} %fusion.23) | copy-start | bytes 12582916
  113.6 4.8 %slice-start = ((f32[128,8192]{1,0:T(8,128)}), f32[64,8192]{1,0:T(8,128)S(1)}, s32[]{:S(2)}) async-start(f32[128,8192]{1,0:T(8,128)} %copy-done.2), calls=%async_computation.3 | async-start | bytes 4194304 | tf_op jit(solution)/shard_map/slice | solution.py:104
  116.1 16.6 %copy-start.10 = (f32[128]{0:T(128)S(1)}, f32[128]{0:T(128)}, u32[]{:S(2)}) copy-start(f32[128]{0:T(128)} %param.9) | copy-start | bytes 1540
  116.1 16.6 %collective-permute-start = (bf16[4096,128]{1,0:T(8,128)(2,1)}, bf16[4096,128]{1,0:T(8,128)(2,1)}, u32[]{:S(2)}, u32[]{:S(2)}) collective-permute-start(bf16[4096,128]{1,0:T(8,128)(2,1)} %convert_element_type.128), channel_id=1, source_target_pairs={{0,32},{32,64},{64,96},{96,128},{128,160},{160,192},{192,224},{224... | collective-permute-start | bytes 3145736 | tf_op jit(solution)/shard_map/ppermute | solution.py:14
  119.9 26.2 %copy-start.3 = (bf16[128,4096]{1,0:T(8,128)(2,1)S(1)}, bf16[128,4096]{1,0:T(8,128)(2,1)}, u32[]{:S(2)}) copy-start(bf16[128,4096]{1,0:T(8,128)(2,1)} %param.5) | copy-start | bytes 3145732
  135.9 38.6 %all-to-all-start.1 = ((bf16[32,128,128]{2,1,0:T(8,128)(2,1)}), bf16[32,128,128]{2,1,0:T(8,128)(2,1)S(1)}, u32[]{:S(2)}, u32[]{:S(2)}) async-start(bf16[32,128,128]{2,1,0:T(8,128)(2,1)} %bitcast.25), calls=%async_computation.1 | async-start | bytes 2097152 | tf_op jit(solution)/shard_map/all_to_all | solution.py:111
Sparse Core Ops, SparseCore 0:
  27.5 40.6 all-gather.1
where the time goes:
time: 185 us; the launch traced here: 184 us
  waiting for transfers between devices  80.5 us (44%)
  local copies, waits for them, and re-layouts  35.4 us (19%)
  starting transfers between devices  25.7 us (14%)
  other arithmetic  16.2 us (9%)
  between operations  13.8 us (7%)
  matrix products  12 us (6%)
    all_gather x1, waiting for transfers between devices, local(): all_taps = lax.all_gather(filter_taps, 'seq', axis=0, tiled=True)  39.4 us
    all_to_all x1, waiting for transfers between devices, local(): lax.all_to_all(filtered, 'wide', split_axis=0, concat_axis=1, tiled=True)  27.7 us
    unnamed x30, local copies, waits for them, and re-layouts  15.6 us
    all_to_all x1, starting transfers between devices, local(): lax.all_to_all(gated_values, 'wide', split_axis=1, concat_axis=0, tiled=T...  13.2 us
    ppermute x1, waiting for transfers between devices, passed_along(): return lax.ppermute(value, axis, pairs)  12.7 us
    all_to_all x1, starting transfers between devices, local(): lax.all_to_all(filtered, 'wide', split_axis=0, concat_axis=1, tiled=True)  10.2 us
    rev x1, local copies, waits for them, and re-layouts, causal_filter(): mirrored = jnp.flip(spectrum[:, row_count // 2:], axis=(1, 2))  6.63 us
    dot_general x1, matrix products, causal_filter(): jnp.einsum('panc,pnqk->qakc', turned, column_block(column_count, 1.0), pr...  4.32 us
  transfers between devices with their start and end apart: 4, of which 3 were waited for; matrix products, arithmetic and copies ran while one was open for 4% of the time, Pallas kernels for 0%

commit v1 on v0

v1 whole, which is shorter than its diff:
```python
import jax
import jax.numpy as jnp
import ml_dtypes
import numpy as np
from jax import lax
from jax.experimental import pallas as pl
from jax.experimental.pallas import tpu as pltpu
from jax.sharding import PartitionSpec as P

MESH = pl.DeviceIdType.MESH
F32, BF16 = jnp.float32, jnp.bfloat16

LANE = 128
BLOCKS = 32
GROUPS = 16
FREQ = 128
WIDE = 64
PITCH = FREQ + 8


def tables():
    k, b, m = np.arange(FREQ), np.arange(LANE), np.arange(WIDE)
    angle = np.pi * (2 * k + 1) / 256
    wide_angle = 2 * np.pi * (np.outer(m, m) % WIDE) / WIDE

    spread = np.outer(angle, b)
    block_in = np.concatenate([np.cos(spread), -np.sin(spread)], 0)
    cosine, sine = np.cos(wide_angle), np.sin(wide_angle)
    wide_in = np.zeros((2, WIDE, WIDE, 2))
    wide_in[0, :, :, 0], wide_in[0, :, :, 1] = cosine, sine
    wide_in[1, :, :, 0], wide_in[1, :, :, 1] = -sine, cosine

    turn = np.exp(-1j * wide_angle)[:, :BLOCKS]
    tap_in = np.zeros((2, 2, WIDE, BLOCKS, 2))
    for parity, sign in ((0, 1.0), (1, -1.0)):
        factor = (1 + 1j * sign * np.exp(-2j * np.pi * m / WIDE))[:, None] * turn
        tap_in[parity, 0, :, :, 0], tap_in[parity, 0, :, :, 1] = factor.real, -factor.imag
        tap_in[parity, 1, :, :, 0], tap_in[parity, 1, :, :, 1] = factor.imag, factor.real

    wide_out = np.zeros((BLOCKS, 2, 2, WIDE))
    cosine, sine = cosine[BLOCKS:], sine[BLOCKS:]
    wide_out[:, 0, 0], wide_out[:, 0, 1] = cosine, -sine
    wide_out[:, 1, 0], wide_out[:, 1, 1] = sine, cosine
    block_out = np.concatenate([np.cos(spread.T), -np.sin(spread.T)], 1)
    made = (
        block_in,
        wide_in.reshape(2 * WIDE, 2 * WIDE),
        tap_in.reshape(2, 2 * WIDE, 2 * BLOCKS),
        wide_out.reshape(2 * BLOCKS, 2 * WIDE) / WIDE,
        block_out / FREQ,
    )
    return [table.astype(np.float32).astype(ml_dtypes.bfloat16) for table in made]


def dot(left, right):
    return jnp.dot(left, right, preferred_element_type=F32)


def rows(start, count=LANE, align=8):
    return pl.ds(pl.multiple_of(start, align), count)


def kernel(
    out_gate, in_gate, values, taps, skip, block_in, wide_in, tap_in, wide_out, block_out,
    result,
    gate_a, gate_b, gate_c, gated, own, before, all_taps, filtered, returned,
    signal_rows, tap_rows, tap_spectrum, product, answer_rows,
    load_sem, go_send, go_recv, pass_send, pass_recv, tap_send, tap_recv, twin_send, twin_recv,
    back_send, back_recv,
):
    s, v = lax.axis_index("seq"), lax.axis_index("wide")
    z, x = v // 4, v % 4
    twin = s + 1 - 2 * (s % 2)

    def ahead(k):
        return (z + k // 4) % 8 * 4 + (x + k % 4) % 4

    def behind(k):
        return (z + 8 - k // 4) % 8 * 4 + (x + 4 - k % 4) % 4

    loads = [
        pltpu.make_async_copy(source, target, load_sem.at[i])
        for i, (source, target) in enumerate(((in_gate, gate_a), (values, gate_b), (out_gate, gate_c)))
    ]
    for load in loads:
        load.start()

    barrier = pltpu.get_barrier_semaphore()

    def greet(k, carry):
        pl.semaphore_signal(barrier, inc=1, device_id={"wide": behind(k)}, device_id_type=MESH)
        return carry

    lax.fori_loop(1, BLOCKS, greet, 0)
    for step in range(1, 8):
        pl.semaphore_signal(
            barrier, inc=1, device_id={"seq": (s + GROUPS - 2 * step) % GROUPS}, device_id_type=MESH
        )
    pl.semaphore_signal(barrier, inc=1, device_id={"seq": twin}, device_id_type=MESH)
    pl.semaphore_signal(barrier, inc=1, device_id={"seq": (s + GROUPS - 1) % GROUPS}, device_id_type=MESH)

    def go(k):
        return pltpu.make_async_remote_copy(
            src_ref=gated.at[ahead(k)], dst_ref=own.at[v],
            send_sem=go_send.at[k], recv_sem=go_recv.at[k],
            device_id={"wide": ahead(k)}, device_id_type=MESH,
        )

    def pass_on(k):
        block = behind(k)
        return pltpu.make_async_remote_copy(
            src_ref=own.at[block], dst_ref=before.at[block],
            send_sem=pass_send.at[k], recv_sem=pass_recv.at[k],
            device_id={"seq": (s + 1) % GROUPS}, device_id_type=MESH,
        )

    def tap_go(i):
        return pltpu.make_async_remote_copy(
            src_ref=all_taps.at[s], dst_ref=all_taps.at[s],
            send_sem=tap_send.at[i], recv_sem=tap_recv.at[i],
            device_id={"seq": (s + 2 * i) % GROUPS}, device_id_type=MESH,
        )

    def tap_twin(i):
        group = (s + GROUPS - 2 * i) % GROUPS
        return pltpu.make_async_remote_copy(
            src_ref=all_taps.at[group], dst_ref=all_taps.at[group],
            send_sem=twin_send.at[i], recv_sem=twin_recv.at[i],
            device_id={"seq": twin}, device_id_type=MESH,
        )

    def back(k):
        return pltpu.make_async_remote_copy(
            src_ref=filtered.at[ahead(k)], dst_ref=returned.at[v],
            send_sem=back_send.at[k], recv_sem=back_recv.at[k],
            device_id={"wide": ahead(k)}, device_id_type=MESH,
        )

    all_taps[s] = taps[...]
    loads[0].wait()
    loads[1].wait()

    def gate(u, carry):
        columns = rows(u * LANE, align=LANE)
        gated[u] = (gate_a[:, columns].astype(F32) * gate_b[:, columns].astype(F32)).astype(BF16)
        return carry

    lax.fori_loop(0, BLOCKS, gate, 0, unroll=2)
    pl.semaphore_wait(barrier, BLOCKS - 1 + 9)

    def send_go(k, carry):
        go(k).start()
        return carry

    lax.fori_loop(1, BLOCKS, send_go, 0)
    tap_twin(0).start()
    for i in range(1, 8):
        tap_go(i).start()
    own[v] = gated[v]

    def block_spectrum(source, target, at):
        spectrum = dot(block_in[...], source)
        target[rows(at * 2 * PITCH), :] = spectrum[:FREQ]
        target[rows(at * 2 * PITCH + PITCH), :] = spectrum[FREQ:]

    pass_on(0).start()
    block_spectrum(own[v], signal_rows, BLOCKS + v)

    def arrive(k, carry):
        go(k).wait_recv()
        pass_on(k).start()
        at = behind(k)
        block_spectrum(own[at], signal_rows, BLOCKS + at)
        return carry

    lax.fori_loop(1, BLOCKS, arrive, 0)

    for i in range(1, 8):
        tap_go(i).wait_recv()
        tap_twin(i).start()
    for i in range(8):
        tap_twin(i).wait_recv()

    def tap_block(g, carry):
        for half in range(2):
            block_spectrum(all_taps[g, half * LANE : (half + 1) * LANE], tap_rows, 2 * g + half)
        return carry

    lax.fori_loop(0, GROUPS, tap_block, 0, unroll=2)

    def pair(source, k, count):
        first = source[pl.ds(k, count, stride=PITCH), :]
        second = source[pl.ds(k + FREQ // 2, count, stride=PITCH), :]
        return jnp.concatenate([first, second], axis=1).astype(BF16)

    def tap_wide(i, carry):
        for p in range(8):
            k = 8 * i + p
            tap_spectrum[k] = dot(tap_in[p % 2], pair(tap_rows, k, 2 * BLOCKS))
        return carry

    lax.fori_loop(0, FREQ // 16, tap_wide, 0)

    def arrive_before(k, carry):
        pass_on(k).wait_recv()
        at = behind(k)
        block = before[at]
        block_spectrum(jnp.where(s > 0, block, jnp.zeros_like(block)), signal_rows, at)
        return carry

    lax.fori_loop(0, BLOCKS, arrive_before, 0)

    def multiply(i, carry):
        for p in range(8):
            k = 8 * i + p
            signal = dot(wide_in[...], pair(signal_rows, k, 2 * WIDE))
            tap = tap_spectrum[k]
            real, imag, tap_real, tap_imag = signal[:WIDE], signal[WIDE:], tap[:WIDE], tap[WIDE:]
            product[k] = jnp.concatenate(
                [real * tap_real - imag * tap_imag, real * tap_imag + imag * tap_real], axis=0
            ).astype(BF16)
        return carry

    lax.fori_loop(0, FREQ // 16, multiply, 0)

    def wide_back(i, carry):
        for p in range(8):
            k = 8 * i + p
            answer = dot(wide_out[...], product[k])
            answer_rows[pl.ds(k, 2 * BLOCKS, stride=PITCH), :] = answer[:, :LANE]
            answer_rows[pl.ds(k + FREQ // 2, 2 * BLOCKS, stride=PITCH), :] = answer[:, LANE:]
        return carry

    lax.fori_loop(0, FREQ // 16, wide_back, 0)

    def finish(i, carry):
        for p in range(4):
            at = ahead(4 * i + p)
            spectrum = jnp.concatenate(
                [answer_rows[rows(at * 2 * PITCH), :], answer_rows[rows(at * 2 * PITCH + PITCH), :]], axis=0
            ).astype(BF16)
            direct = skip[...] * own[at].astype(F32)
            filtered[at] = (dot(block_out[...], spectrum) + direct).astype(BF16)
        for p in range(4):
            @pl.when(4 * i + p > 0)
            def _():
                back(4 * i + p).start()
        return carry

    lax.fori_loop(0, BLOCKS // 4, finish, 0)
    loads[2].wait()
    returned[v] = filtered[v]

    def output(at):
        columns = rows(at * LANE, align=LANE)
        result[:, columns] = (gate_c[:, columns].astype(F32) * returned[at].astype(F32)).astype(BF16)

    output(v)

    def arrive_back(k, carry):
        back(k).wait_recv()
        output(behind(k))
        return carry

    lax.fori_loop(1, BLOCKS, arrive_back, 0)

    def drain(k, carry):
        go(k).wait_send()
        back(k).wait_send()
        pass_on(k).wait_send()
        return carry

    lax.fori_loop(1, BLOCKS, drain, 0)
    pass_on(0).wait_send()
    for i in range(8):
        tap_twin(i).wait_send()
    for i in range(1, 8):
        tap_go(i).wait_send()


def local(out_gate, in_gate, values, filter_taps, skip_gain):
    vmem, anywhere = pl.BlockSpec(memory_space=pltpu.VMEM), pl.BlockSpec(memory_space=pl.ANY)
    block = (BLOCKS, LANE, LANE)
    many, eight = pltpu.SemaphoreType.DMA((BLOCKS,)), pltpu.SemaphoreType.DMA((8,))
    return pl.pallas_call(
        kernel,
        out_shape=jax.ShapeDtypeStruct(out_gate.shape, BF16),
        in_specs=[anywhere] * 3 + [vmem] * 7,
        out_specs=vmem,
        scratch_shapes=[pltpu.VMEM(out_gate.shape, BF16)] * 3
        + [pltpu.VMEM(block, BF16)] * 3
        + [pltpu.VMEM((GROUPS, 2 * LANE, LANE), BF16)]
        + [pltpu.VMEM(block, BF16)] * 2
        + [
            pltpu.VMEM((2 * WIDE * PITCH, LANE), F32),
            pltpu.VMEM((2 * BLOCKS * PITCH, LANE), F32),
            pltpu.VMEM((FREQ // 2, 2 * WIDE, 2 * LANE), F32),
            pltpu.VMEM((FREQ // 2, 2 * WIDE, 2 * LANE), BF16),
            pltpu.VMEM((2 * BLOCKS * PITCH, LANE), F32),
            pltpu.SemaphoreType.DMA((3,)),
            many, many, many, many, eight, eight, eight, eight, many, many,
        ],
        compiler_params=pltpu.CompilerParams(
            collective_id=0, has_side_effects=True, vmem_limit_bytes=58 << 20
        ),
    )(out_gate, in_gate, values, filter_taps, skip_gain[None, :], *tables())


def solution(mesh):
    rows_split = P(("seq", "wide"), None)
    return jax.shard_map(
        local,
        mesh=mesh,
        in_specs=(rows_split, rows_split, rows_split, P("seq", "wide"), P("wide")),
        out_specs=rows_split,
        check_vma=False,
    )
```

time: 185 us -> 89 us (0.48)
  the two profiles are of different devices: /device:TPU:16 before, /device:TPU:1 now
where the time goes in v1:
time: 89 us; the launch traced here: 88.8 us
  Pallas kernels  86.5 us (97%)
  local copies, waits for them, and re-layouts  2.29 us (3%)
    pallas_call x1, Pallas kernels, local(): pl.pallas_call(kernel, out_shape=jax.ShapeDtypeStruct(out_gate.shape, BF1...  86.5 us
    unnamed x1, local copies, waits for them, and re-layouts  2.29 us

profile of v1, /device:TPU:1, one launch (start us, length us, event | category | flops | bytes accessed | tf_op | source)
XLA Modules:
  0.0 88.8 jit_solution(11097719903193990466)
XLA Ops:
  0.0 86.5 %shard_map.100 = bf16[128,4096]{1,0:T(8,128)(2,1)} custom-call(bf16[128,4096]{1,0:T(8,128)(2,1)} %out_gate.1, bf16[128,4096]{1,0:T(8,128)(2,1)} %in_gate.1, bf16[128,4096]{1,0:T(8,128)(2,1)} %values.1, bf16[256,128]{1,0:T(8,128)(2,1)} %taps.1, f32[1,128]{1,0:T(1,128)} %bitcast.1, bf16[256,128]{1,0:T(8,128)(2,1)} %constant.10.clone.block_in, ...), custom_call_target="tpu_custom_call" | custom-call | tf_op jit(solution)/shard_map/pallas_call | solution.py:285
  86.5 2.3 %copy.12 = bf16[128,4096]{1,0:T(8,128)(2,1)} copy(bf16[128,4096]{1,0:T(8,128)(2,1)} %shard_map.100) | data formatting | bytes 2097152

commit v2 on v1

--- a/solution.py
+++ b/solution.py
@@ -15,6 +15,7 @@
 GROUPS = 16
 FREQ = 128
 WIDE = 64
+LAG = 5
 PITCH = FREQ + 8
 
 
@@ -61,26 +62,35 @@
 
 
 def kernel(
-    out_gate, in_gate, values, taps, skip, block_in, wide_in, tap_in, wide_out, block_out,
-    result,
-    gate_a, gate_b, gate_c, gated, own, before, all_taps, filtered, returned,
-    signal_rows, tap_rows, tap_spectrum, product, answer_rows,
-    load_sem, go_send, go_recv, pass_send, pass_recv, tap_send, tap_recv, twin_send, twin_recv,
-    back_send, back_recv,
+    in_gate, values, taps, skip, *rest
 ):
+    table_refs, rest = rest[:5], rest[5:]
+    result, gate_a, gate_b, skip_here, *rest = rest
+    (block_in, wide_in, tap_in, wide_out, block_out), rest = rest[:5], rest[5:]
+    (
+        gated, own, before, all_taps, filtered, returned,
+        signal_rows, tap_rows, tap_spectrum, product, answer_rows,
+        load_sem, go_send, go_recv, pass_send, pass_recv, tap_send, tap_recv, twin_send, twin_recv,
+        back_send, back_recv,
+    ) = rest
     s, v = lax.axis_index("seq"), lax.axis_index("wide")
     z, x = v // 4, v % 4
     twin = s + 1 - 2 * (s % 2)
 
+    def near(i):
+        return (8 + (2 * (i % 2) - 1) * ((i + 1) // 2)) % 8
+
     def ahead(k):
         return (z + k // 4) % 8 * 4 + (x + k % 4) % 4
 
     def behind(k):
         return (z + 8 - k // 4) % 8 * 4 + (x + 4 - k % 4) % 4
 
+    here = (in_gate, values, taps, *table_refs, skip)
+    there = (gate_a, gate_b, all_taps.at[s], block_in, wide_in, tap_in, wide_out, block_out, skip_here)
     loads = [
         pltpu.make_async_copy(source, target, load_sem.at[i])
-        for i, (source, target) in enumerate(((in_gate, gate_a), (values, gate_b), (out_gate, gate_c)))
+        for i, (source, target) in enumerate(zip(here, there))
     ]
     for load in loads:
         load.start()
@@ -106,11 +116,11 @@
             device_id={"wide": ahead(k)}, device_id_type=MESH,
         )
 
-    def pass_on(k):
-        block = behind(k)
-        return pltpu.make_async_remote_copy(
-            src_ref=own.at[block], dst_ref=before.at[block],
-            send_sem=pass_send.at[k], recv_sem=pass_recv.at[k],
+    def pass_on(step):
+        blocks = pl.ds((z + 8 - step) % 8 * 4, 4)
+        return pltpu.make_async_remote_copy(
+            src_ref=own.at[blocks], dst_ref=before.at[blocks],
+            send_sem=pass_send.at[step], recv_sem=pass_recv.at[step],
             device_id={"seq": (s + 1) % GROUPS}, device_id_type=MESH,
         )
 
@@ -136,44 +146,44 @@
             device_id={"wide": ahead(k)}, device_id_type=MESH,
         )
 
-    all_taps[s] = taps[...]
+    pl.semaphore_wait(barrier, BLOCKS - 1 + 9)
+    loads[2].wait()
+    for i in range(1, 8):
+        tap_go(i).start()
+    tap_twin(0).start()
     loads[0].wait()
     loads[1].wait()
 
-    def gate(u, carry):
+    def gate(u):
         columns = rows(u * LANE, align=LANE)
         gated[u] = (gate_a[:, columns].astype(F32) * gate_b[:, columns].astype(F32)).astype(BF16)
-        return carry
-
-    lax.fori_loop(0, BLOCKS, gate, 0, unroll=2)
-    pl.semaphore_wait(barrier, BLOCKS - 1 + 9)
-
-    def send_go(k, carry):
-        go(k).start()
-        return carry
-
-    lax.fori_loop(1, BLOCKS, send_go, 0)
-    tap_twin(0).start()
-    for i in range(1, 8):
-        tap_go(i).start()
+
+    def send_go(i, carry):
+        step = near(i)
+        for j in range(4):
+            k = 4 * step + j
+            gate(ahead(k))
+
+            @pl.when(k > 0)
+            def _():
+                go(k).start()
+
+        return carry
+
+    lax.fori_loop(0, 8, send_go, 0)
     own[v] = gated[v]
+    for load in loads[3:]:
+        load.wait()
 
     def block_spectrum(source, target, at):
         spectrum = dot(block_in[...], source)
         target[rows(at * 2 * PITCH), :] = spectrum[:FREQ]
         target[rows(at * 2 * PITCH + PITCH), :] = spectrum[FREQ:]
 
-    pass_on(0).start()
-    block_spectrum(own[v], signal_rows, BLOCKS + v)
-
-    def arrive(k, carry):
-        go(k).wait_recv()
-        pass_on(k).start()
-        at = behind(k)
-        block_spectrum(own[at], signal_rows, BLOCKS + at)
-        return carry
-
-    lax.fori_loop(1, BLOCKS, arrive, 0)
+    def pair(source, k, count):
+        first = source[pl.ds(k, count, stride=PITCH), :]
+        second = source[pl.ds(k + FREQ // 2, count, stride=PITCH), :]
+        return jnp.concatenate([first, second], axis=1).astype(BF16)
 
     for i in range(1, 8):
         tap_go(i).wait_recv()
@@ -181,38 +191,61 @@
     for i in range(8):
         tap_twin(i).wait_recv()
 
-    def tap_block(g, carry):
-        for half in range(2):
-            block_spectrum(all_taps[g, half * LANE : (half + 1) * LANE], tap_rows, 2 * g + half)
-        return carry
-
-    lax.fori_loop(0, GROUPS, tap_block, 0, unroll=2)
-
-    def pair(source, k, count):
-        first = source[pl.ds(k, count, stride=PITCH), :]
-        second = source[pl.ds(k + FREQ // 2, count, stride=PITCH), :]
-        return jnp.concatenate([first, second], axis=1).astype(BF16)
+    def tap_block(i, carry):
+        for j in range(4):
+            block = all_taps[2 * i + j // 2, j % 2 * LANE : (j % 2 + 1) * LANE]
+            block_spectrum(block, tap_rows, 4 * i + j)
+        return carry
+
+    lax.fori_loop(0, 8, tap_block, 0)
 
     def tap_wide(i, carry):
-        for p in range(8):
-            k = 8 * i + p
+        for p in range(16):
+            k = 16 * i + p
             tap_spectrum[k] = dot(tap_in[p % 2], pair(tap_rows, k, 2 * BLOCKS))
         return carry
 
-    lax.fori_loop(0, FREQ // 16, tap_wide, 0)
-
-    def arrive_before(k, carry):
-        pass_on(k).wait_recv()
-        at = behind(k)
-        block = before[at]
-        block_spectrum(jnp.where(s > 0, block, jnp.zeros_like(block)), signal_rows, at)
-        return carry
-
-    lax.fori_loop(0, BLOCKS, arrive_before, 0)
+    lax.fori_loop(0, 4, tap_wide, 0)
+
+    def arrive(i):
+        step = near(i)
+        for j in range(4):
+            @pl.when(4 * step + j > 0)
+            def _():
+                go(4 * step + j).wait_recv()
+        pass_on(step).start()
+        for j in range(4):
+            at = (z + 8 - step) % 8 * 4 + j
+            block_spectrum(own[at], signal_rows, BLOCKS + at)
+
+    def arrive_before(i):
+        step = near(i)
+        pass_on(step).wait_recv()
+        for j in range(4):
+            at = (z + 8 - step) % 8 * 4 + j
+            block = before[at]
+            block_spectrum(jnp.where(s > 0, block, jnp.zeros_like(block)), signal_rows, at)
+
+    def first(i, carry):
+        arrive(i)
+        return carry
+
+    def both(i, carry):
+        arrive(i)
+        arrive_before(i - LAG)
+        return carry
+
+    def last(i, carry):
+        arrive_before(i)
+        return carry
+
+    lax.fori_loop(0, LAG, first, 0)
+    lax.fori_loop(LAG, 8, both, 0)
+    lax.fori_loop(8 - LAG, 8, last, 0)
 
     def multiply(i, carry):
-        for p in range(8):
-            k = 8 * i + p
+        for p in range(32):
+            k = 32 * i + p
             signal = dot(wide_in[...], pair(signal_rows, k, 2 * WIDE))
             tap = tap_spectrum[k]
             real, imag, tap_real, tap_imag = signal[:WIDE], signal[WIDE:], tap[:WIDE], tap[WIDE:]
@@ -221,57 +254,63 @@
             ).astype(BF16)
         return carry
 
-    lax.fori_loop(0, FREQ // 16, multiply, 0)
+    lax.fori_loop(0, 2, multiply, 0)
 
     def wide_back(i, carry):
-        for p in range(8):
-            k = 8 * i + p
+        for p in range(16):
+            k = 16 * i + p
             answer = dot(wide_out[...], product[k])
             answer_rows[pl.ds(k, 2 * BLOCKS, stride=PITCH), :] = answer[:, :LANE]
             answer_rows[pl.ds(k + FREQ // 2, 2 * BLOCKS, stride=PITCH), :] = answer[:, LANE:]
         return carry
 
-    lax.fori_loop(0, FREQ // 16, wide_back, 0)
+    lax.fori_loop(0, 4, wide_back, 0)
 
     def finish(i, carry):
         for p in range(4):
-            at = ahead(4 * i + p)
+            at = ahead(4 * near(i) + p)
             spectrum = jnp.concatenate(
                 [answer_rows[rows(at * 2 * PITCH), :], answer_rows[rows(at * 2 * PITCH + PITCH), :]], axis=0
             ).astype(BF16)
-            direct = skip[...] * own[at].astype(F32)
+            direct = skip_here[...] * own[at].astype(F32)
             filtered[at] = (dot(block_out[...], spectrum) + direct).astype(BF16)
         for p in range(4):
-            @pl.when(4 * i + p > 0)
+            k = 4 * near(i) + p
+
+            @pl.when(k > 0)
             def _():
-                back(4 * i + p).start()
+                back(k).start()
         return carry
 
     lax.fori_loop(0, BLOCKS // 4, finish, 0)
-    loads[2].wait()
     returned[v] = filtered[v]
 
     def output(at):
         columns = rows(at * LANE, align=LANE)
-        result[:, columns] = (gate_c[:, columns].astype(F32) * returned[at].astype(F32)).astype(BF16)
-
-    output(v)
-
-    def arrive_back(k, carry):
-        back(k).wait_recv()
-        output(behind(k))
-        return carry
-
-    lax.fori_loop(1, BLOCKS, arrive_back, 0)
+        result[:, columns] = returned[at]
+
+    def arrive_back(i, carry):
+        for j in range(4):
+            k = 4 * near(i) + j
+
+            @pl.when(k > 0)
+            def _():
+                back(k).wait_recv()
+
+        for j in range(4):
+            output(behind(4 * near(i) + j))
+        return carry
+
+    lax.fori_loop(0, 8, arrive_back, 0)
 
     def drain(k, carry):
         go(k).wait_send()
         back(k).wait_send()
-        pass_on(k).wait_send()
         return carry
 
     lax.fori_loop(1, BLOCKS, drain, 0)
-    pass_on(0).wait_send()
+    for i in range(8):
+        pass_on(i).wait_send()
     for i in range(8):
         tap_twin(i).wait_send()
     for i in range(1, 8):
@@ -282,12 +321,15 @@
     vmem, anywhere = pl.BlockSpec(memory_space=pltpu.VMEM), pl.BlockSpec(memory_space=pl.ANY)
     block = (BLOCKS, LANE, LANE)
     many, eight = pltpu.SemaphoreType.DMA((BLOCKS,)), pltpu.SemaphoreType.DMA((8,))
-    return pl.pallas_call(
+    made = tables()
+    filtered = pl.pallas_call(
         kernel,
         out_shape=jax.ShapeDtypeStruct(out_gate.shape, BF16),
-        in_specs=[anywhere] * 3 + [vmem] * 7,
+        in_specs=[anywhere] * (4 + len(made)),
         out_specs=vmem,
-        scratch_shapes=[pltpu.VMEM(out_gate.shape, BF16)] * 3
+        scratch_shapes=[pltpu.VMEM(out_gate.shape, BF16)] * 2
+        + [pltpu.VMEM((1, LANE), F32)]
+        + [pltpu.VMEM(table.shape, BF16) for table in made]
         + [pltpu.VMEM(block, BF16)] * 3
         + [pltpu.VMEM((GROUPS, 2 * LANE, LANE), BF16)]
         + [pltpu.VMEM(block, BF16)] * 2
@@ -297,13 +339,14 @@
             pltpu.VMEM((FREQ // 2, 2 * WIDE, 2 * LANE), F32),
             pltpu.VMEM((FREQ // 2, 2 * WIDE, 2 * LANE), BF16),
             pltpu.VMEM((2 * BLOCKS * PITCH, LANE), F32),
-            pltpu.SemaphoreType.DMA((3,)),
-            many, many, many, many, eight, eight, eight, eight, many, many,
+            pltpu.SemaphoreType.DMA((4 + len(made),)),
+            many, many, eight, eight, eight, eight, eight, eight, many, many,
         ],
         compiler_params=pltpu.CompilerParams(
             collective_id=0, has_side_effects=True, vmem_limit_bytes=58 << 20
         ),
-    )(out_gate, in_gate, values, filter_taps, skip_gain[None, :], *tables())
+    )(in_gate, values, filter_taps, skip_gain[None, :], *made)
+    return (out_gate.astype(F32) * filtered.astype(F32)).astype(BF16)
 
 
 def solution(mesh):

time: 89 us -> 78.2 us (0.88)
  the two profiles are of different devices: /device:TPU:1 before, /device:TPU:8 now
where the time goes in v2:
time: 78.2 us; the launch traced here: 78.1 us
  Pallas kernels  75.6 us (97%)
  other arithmetic  2.45 us (3%)
    pallas_call x1, Pallas kernels, local(): pl.pallas_call(kernel, out_shape=jax.ShapeDtypeStruct(out_gate.shape, BF1...  75.6 us
    convert_element_type x1, other arithmetic, local(): return (out_gate.astype(F32) * filtered.astype(F32)).astype(BF16)  2.45 us

profile of v2, /device:TPU:8, one launch (start us, length us, event | category | flops | bytes accessed | tf_op | source)
XLA Modules:
  0.0 78.1 jit_solution(11266109543780116626)
XLA Ops:
  0.0 0.0 copy-start
  0.0 75.6 %shard_map.100 = bf16[128,4096]{1,0:T(8,128)(2,1)} custom-call(bf16[128,4096]{1,0:T(8,128)(2,1)} %in_gate.1, bf16[128,4096]{1,0:T(8,128)(2,1)} %values.1, bf16[256,128]{1,0:T(8,128)(2,1)} %taps.1, f32[1,128]{1,0:T(1,128)} %bitcast.1, bf16[256,128]{1,0:T(8,128)(2,1)} %constant.10.clone.rest_0_, bf16[128,128]{1,0:T(8,128)(2,1)} %constant.11.clone.rest_1_, ...), custom_call_target="tpu_custom_call" | custom-call | tf_op jit(solution)/shard_map/pallas_call | solution.py:325
  75.7 0.0 copy-done
  75.7 2.4 %multiply_convert_fusion = bf16[128,4096]{1,0:T(8,128)(2,1)} fusion(bf16[128,4096]{1,0:T(8,128)(2,1)} %shard_map.100, bf16[128,4096]{1,0:T(8,128)(2,1)S(1)} %copy-done), kind=kLoop, calls=%fused_computation | loop fusion | flops 2097152 | bytes 3145728 | tf_op jit(solution)/shard_map/convert_element_type | solution.py:349
Async XLA Ops:
  0.0 75.7 %copy-start = (bf16[128,4096]{1,0:T(8,128)(2,1)S(1)}, bf16[128,4096]{1,0:T(8,128)(2,1)}, u32[]{:S(2)}) copy-start(bf16[128,4096]{1,0:T(8,128)(2,1)} %param.10) | copy-start | bytes 3145732

commit v3 on v2

--- a/solution.py
+++ b/solution.py
@@ -62,16 +62,16 @@
 
 
 def kernel(
-    in_gate, values, taps, skip, *rest
+    in_gate, values, taps, skip, out_gate, *rest
 ):
     table_refs, rest = rest[:5], rest[5:]
-    result, gate_a, gate_b, skip_here, *rest = rest
+    result, gate_a, gate_b, gate_c, mixed, skip_here, *rest = rest
     (block_in, wide_in, tap_in, wide_out, block_out), rest = rest[:5], rest[5:]
     (
         gated, own, before, all_taps, filtered, returned,
         signal_rows, tap_rows, tap_spectrum, product, answer_rows,
         load_sem, go_send, go_recv, pass_send, pass_recv, tap_send, tap_recv, twin_send, twin_recv,
-        back_send, back_recv,
+        back_send, back_recv, out_sem,
     ) = rest
     s, v = lax.axis_index("seq"), lax.axis_index("wide")
     z, x = v // 4, v % 4
@@ -86,8 +86,8 @@
     def behind(k):
         return (z + 8 - k // 4) % 8 * 4 + (x + 4 - k % 4) % 4
 
-    here = (in_gate, values, taps, *table_refs, skip)
-    there = (gate_a, gate_b, all_taps.at[s], block_in, wide_in, tap_in, wide_out, block_out, skip_here)
+    here = (in_gate, values, taps, *table_refs, skip, out_gate)
+    there = (gate_a, gate_b, all_taps.at[s], block_in, wide_in, tap_in, wide_out, block_out, skip_here, gate_c)
     loads = [
         pltpu.make_async_copy(source, target, load_sem.at[i])
         for i, (source, target) in enumerate(zip(here, there))
@@ -102,12 +102,8 @@
         return carry
 
     lax.fori_loop(1, BLOCKS, greet, 0)
-    for step in range(1, 8):
-        pl.semaphore_signal(
-            barrier, inc=1, device_id={"seq": (s + GROUPS - 2 * step) % GROUPS}, device_id_type=MESH
-        )
-    pl.semaphore_signal(barrier, inc=1, device_id={"seq": twin}, device_id_type=MESH)
-    pl.semaphore_signal(barrier, inc=1, device_id={"seq": (s + GROUPS - 1) % GROUPS}, device_id_type=MESH)
+    for other in ((s + GROUPS - 2) % GROUPS, (s + 2) % GROUPS, twin, (s + GROUPS - 1) % GROUPS):
+        pl.semaphore_signal(barrier, inc=1, device_id={"seq": other}, device_id_type=MESH)
 
     def go(k):
         return pltpu.make_async_remote_copy(
@@ -124,17 +120,22 @@
             device_id={"seq": (s + 1) % GROUPS}, device_id_type=MESH,
         )
 
+    def tap_group(i):
+        return (s + (GROUPS - 2 * i if i <= 4 else 2 * (i - 4))) % GROUPS
+
     def tap_go(i):
-        return pltpu.make_async_remote_copy(
-            src_ref=all_taps.at[s], dst_ref=all_taps.at[s],
+        away = 2 if i <= 4 else GROUPS - 2
+        held = all_taps.at[(tap_group(i) + away) % GROUPS]
+        return pltpu.make_async_remote_copy(
+            src_ref=held, dst_ref=held,
             send_sem=tap_send.at[i], recv_sem=tap_recv.at[i],
-            device_id={"seq": (s + 2 * i) % GROUPS}, device_id_type=MESH,
+            device_id={"seq": (s + away) % GROUPS}, device_id_type=MESH,
         )
 
     def tap_twin(i):
-        group = (s + GROUPS - 2 * i) % GROUPS
-        return pltpu.make_async_remote_copy(
-            src_ref=all_taps.at[group], dst_ref=all_taps.at[group],
+        held = all_taps.at[tap_group(i)]
+        return pltpu.make_async_remote_copy(
+            src_ref=held, dst_ref=held,
             send_sem=twin_send.at[i], recv_sem=twin_recv.at[i],
             device_id={"seq": twin}, device_id_type=MESH,
         )
@@ -146,10 +147,10 @@
             device_id={"wide": ahead(k)}, device_id_type=MESH,
         )
 
-    pl.semaphore_wait(barrier, BLOCKS - 1 + 9)
+    pl.semaphore_wait(barrier, BLOCKS - 1 + 4)
     loads[2].wait()
-    for i in range(1, 8):
-        tap_go(i).start()
+    tap_go(1).start()
+    tap_go(5).start()
     tap_twin(0).start()
     loads[0].wait()
     loads[1].wait()
@@ -185,8 +186,10 @@
         second = source[pl.ds(k + FREQ // 2, count, stride=PITCH), :]
         return jnp.concatenate([first, second], axis=1).astype(BF16)
 
-    for i in range(1, 8):
+    for i in (1, 5, 2, 6, 3, 7, 4):
         tap_go(i).wait_recv()
+        if i not in (4, 7):
+            tap_go(i + 1).start()
         tap_twin(i).start()
     for i in range(8):
         tap_twin(i).wait_recv()
@@ -287,47 +290,60 @@
 
     def output(at):
         columns = rows(at * LANE, align=LANE)
-        result[:, columns] = returned[at]
-
-    def arrive_back(i, carry):
-        for j in range(4):
-            k = 4 * near(i) + j
-
-            @pl.when(k > 0)
-            def _():
-                back(k).wait_recv()
-
-        for j in range(4):
-            output(behind(4 * near(i) + j))
-        return carry
-
-    lax.fori_loop(0, 8, arrive_back, 0)
+        mixed[:, columns] = (gate_c[:, columns].astype(F32) * returned[at].astype(F32)).astype(BF16)
 
     def drain(k, carry):
         go(k).wait_send()
-        back(k).wait_send()
         return carry
 
     lax.fori_loop(1, BLOCKS, drain, 0)
     for i in range(8):
         pass_on(i).wait_send()
-    for i in range(8):
         tap_twin(i).wait_send()
     for i in range(1, 8):
         tap_go(i).wait_send()
 
+    def write(i):
+        columns = rows((z + 8 - near(i)) % 8 * 4 * LANE, 4 * LANE, LANE)
+        return pltpu.make_async_copy(mixed.at[:, columns], result.at[:, columns], out_sem.at[i])
+
+    def arrive_back(i, carry):
+        for j in range(4):
+            k = 4 * near(i) + j
+
+            @pl.when(k > 0)
+            def _():
+                back(k).wait_recv()
+
+        for j in range(4):
+            output(behind(4 * near(i) + j))
+        write(i).start()
+        for j in range(4):
+            k = 4 * near(i) + j
+
+            @pl.when(k > 0)
+            def _():
+                back(k).wait_send()
+
+        return carry
+
+    lax.fori_loop(0, 8, arrive_back, 0)
+
+    for i in range(8):
+        write(i).wait()
+
 
 def local(out_gate, in_gate, values, filter_taps, skip_gain):
-    vmem, anywhere = pl.BlockSpec(memory_space=pltpu.VMEM), pl.BlockSpec(memory_space=pl.ANY)
+    anywhere = pl.BlockSpec(memory_space=pl.ANY)
     block = (BLOCKS, LANE, LANE)
     many, eight = pltpu.SemaphoreType.DMA((BLOCKS,)), pltpu.SemaphoreType.DMA((8,))
     made = tables()
-    filtered = pl.pallas_call(
+    mixed = pl.pallas_call(
         kernel,
         out_shape=jax.ShapeDtypeStruct(out_gate.shape, BF16),
-        in_specs=[anywhere] * (4 + len(made)),
-        out_specs=vmem,
-        scratch_shapes=[pltpu.VMEM(out_gate.shape, BF16)] * 2
+        in_specs=[anywhere] * (5 + len(made)),
+        out_specs=anywhere,
+        scratch_shapes=[pltpu.VMEM(out_gate.shape, BF16)] * 4
         + [pltpu.VMEM((1, LANE), F32)]
         + [pltpu.VMEM(table.shape, BF16) for table in made]
         + [pltpu.VMEM(block, BF16)] * 3
@@ -339,14 +355,14 @@
             pltpu.VMEM((FREQ // 2, 2 * WIDE, 2 * LANE), F32),
             pltpu.VMEM((FREQ // 2, 2 * WIDE, 2 * LANE), BF16),
             pltpu.VMEM((2 * BLOCKS * PITCH, LANE), F32),
-            pltpu.SemaphoreType.DMA((4 + len(made),)),
-            many, many, eight, eight, eight, eight, eight, eight, many, many,
+            pltpu.SemaphoreType.DMA((5 + len(made),)),
+            many, many, eight, eight, eight, eight, eight, eight, many, many, eight,
         ],
         compiler_params=pltpu.CompilerParams(
             collective_id=0, has_side_effects=True, vmem_limit_bytes=58 << 20
         ),
-    )(in_gate, values, filter_taps, skip_gain[None, :], *made)
-    return (out_gate.astype(F32) * filtered.astype(F32)).astype(BF16)
+    )(in_gate, values, filter_taps, skip_gain[None, :], out_gate, *made)
+    return mixed
 
 
 def solution(mesh):

time: 78.2 us -> 76.8 us (0.982)
  other arithmetic: 2.45 us -> 0 us
  local copies, waits for them, and re-layouts: 0.01 us -> 2.29 us
  Pallas kernels: 75.6 us -> 73.9 us
    convert_element_type x1 -> x0, other arithmetic: 2.45 us -> none  [local(): return (out_gate.astype(F32) * filtered.astype(F32)).astype(BF16)]
    unnamed x2 -> x1, local copies, waits for them, and re-layouts: 0.01 us -> 2.29 us
    pallas_call x1, Pallas kernels: 75.6 us -> 73.9 us  [local(): pl.pallas_call(kernel, out_shape=jax.ShapeDtypeStruct(out_gate.shape, BF1...]
where the time goes in v3:
time: 76.8 us; the launch traced here: 76.2 us
  Pallas kernels  73.9 us (96%)
  local copies, waits for them, and re-layouts  2.29 us (3%)
    pallas_call x1, Pallas kernels, local(): pl.pallas_call(kernel, out_shape=jax.ShapeDtypeStruct(out_gate.shape, BF1...  73.9 us
    unnamed x1, local copies, waits for them, and re-layouts  2.29 us

profile of v3, /device:TPU:8, one launch (start us, length us, event | category | flops | bytes accessed | tf_op | source)
XLA Modules:
  0.0 76.2 jit_solution(8192267625236767778)
XLA Ops:
  0.0 73.9 %shard_map.100 = bf16[128,4096]{1,0:T(8,128)(2,1)} custom-call(bf16[128,4096]{1,0:T(8,128)(2,1)} %in_gate.1, bf16[128,4096]{1,0:T(8,128)(2,1)} %values.1, bf16[256,128]{1,0:T(8,128)(2,1)} %taps.1, f32[1,128]{1,0:T(1,128)} %bitcast.1, bf16[128,4096]{1,0:T(8,128)(2,1)} %out_gate.1, bf16[256,128]{1,0:T(8,128)(2,1)} %constant.10.clone.rest_0_, ...), custom_call_target="tpu_custom_call" | custom-call | tf_op jit(solution)/shard_map/pallas_call | solution.py:341
  73.9 2.3 %copy.12 = bf16[128,4096]{1,0:T(8,128)(2,1)} copy(bf16[128,4096]{1,0:T(8,128)(2,1)} %shard_map.100) | data formatting | bytes 2097152

commit v4 on v3

--- a/solution.py
+++ b/solution.py
@@ -15,7 +15,7 @@
 GROUPS = 16
 FREQ = 128
 WIDE = 64
-LAG = 5
+LAG = 6
 PITCH = FREQ + 8
 
 
@@ -81,10 +81,10 @@
         return (8 + (2 * (i % 2) - 1) * ((i + 1) // 2)) % 8
 
     def ahead(k):
-        return (z + k // 4) % 8 * 4 + (x + k % 4) % 4
+        return lax.rem(z + k // 4, 8) * 4 + lax.rem(x + k % 4, 4)
 
     def behind(k):
-        return (z + 8 - k // 4) % 8 * 4 + (x + 4 - k % 4) % 4
+        return lax.rem(z + 8 - k // 4, 8) * 4 + lax.rem(x + 4 - k % 4, 4)
 
     here = (in_gate, values, taps, *table_refs, skip, out_gate)
     there = (gate_a, gate_b, all_taps.at[s], block_in, wide_in, tap_in, wide_out, block_out, skip_here, gate_c)
@@ -97,11 +97,8 @@
 
     barrier = pltpu.get_barrier_semaphore()
 
-    def greet(k, carry):
+    for k in range(1, BLOCKS):
         pl.semaphore_signal(barrier, inc=1, device_id={"wide": behind(k)}, device_id_type=MESH)
-        return carry
-
-    lax.fori_loop(1, BLOCKS, greet, 0)
     for other in ((s + GROUPS - 2) % GROUPS, (s + 2) % GROUPS, twin, (s + GROUPS - 1) % GROUPS):
         pl.semaphore_signal(barrier, inc=1, device_id={"seq": other}, device_id_type=MESH)
 
@@ -159,19 +156,11 @@
         columns = rows(u * LANE, align=LANE)
         gated[u] = (gate_a[:, columns].astype(F32) * gate_b[:, columns].astype(F32)).astype(BF16)
 
-    def send_go(i, carry):
-        step = near(i)
-        for j in range(4):
-            k = 4 * step + j
+    for i in range(8):
+        for k in range(4 * (0, 1, 7, 2, 6, 3, 5, 4)[i], 4 * (0, 1, 7, 2, 6, 3, 5, 4)[i] + 4):
             gate(ahead(k))
-
-            @pl.when(k > 0)
-            def _():
+            if k > 0:
                 go(k).start()
-
-        return carry
-
-    lax.fori_loop(0, 8, send_go, 0)
     own[v] = gated[v]
     for load in loads[3:]:
         load.wait()

time: 76.8 us -> 76.3 us (level)
  the two profiles are of different devices: /device:TPU:8 before, /device:TPU:96 now
where the time goes in v4:
time: 76.3 us; the launch traced here: 76.1 us
  Pallas kernels  73.8 us (97%)
  local copies, waits for them, and re-layouts  2.29 us (3%)
    pallas_call x1, Pallas kernels, local(): pl.pallas_call(kernel, out_shape=jax.ShapeDtypeStruct(out_gate.shape, BF1...  73.8 us
    unnamed x1, local copies, waits for them, and re-layouts  2.29 us

profile of v4, /device:TPU:96, one launch (start us, length us, event | category | flops | bytes accessed | tf_op | source)
XLA Modules:
  0.0 76.1 jit_solution(7967474742990356226)
XLA Ops:
  0.0 73.8 %shard_map.100 = bf16[128,4096]{1,0:T(8,128)(2,1)} custom-call(bf16[128,4096]{1,0:T(8,128)(2,1)} %in_gate.1, bf16[128,4096]{1,0:T(8,128)(2,1)} %values.1, bf16[256,128]{1,0:T(8,128)(2,1)} %taps.1, f32[1,128]{1,0:T(1,128)} %bitcast.1, bf16[128,4096]{1,0:T(8,128)(2,1)} %out_gate.1, bf16[256,128]{1,0:T(8,128)(2,1)} %constant.10.clone.rest_0_, ...), custom_call_target="tpu_custom_call" | custom-call | tf_op jit(solution)/shard_map/pallas_call | solution.py:330
  73.9 2.3 %copy.12 = bf16[128,4096]{1,0:T(8,128)(2,1)} copy(bf16[128,4096]{1,0:T(8,128)(2,1)} %shard_map.100) | data formatting | bytes 2097152
